TPU v7x, 32 devices: a whole 2x2x4 slice. The times are simulated.
32 devices in a mesh: grp: 2 (over x), lon: 16 (over z, y, core).
Axes of the slice: x: 2, y: 2, z: 4, core: 2. Of those that a mesh axis runs over, the one named last changes fastest.
Arguments:
- trajectory: bfloat16 [1280, 4, 4, 8, 192], P(('grp', 'lon')), parts along dimension 0, may hold values from -6 to 6
- lat_order: int32 [640], replicated, may hold values from 0 to 639, each once
- basis: float32 [8, 8, 192, 640], P('grp', None, 'lon'), parts along dimension 0, may hold values from -80 to 80, as said below
- weight: float32 [8, 640], replicated, may hold values from 0.3 to 3
Outputs:
- next_vector: float32 [16, 192, 640], P('grp', 'lon'), parts along dimension 0
- coefficients: float32 [10], P('grp'), parts along dimension 0
There are 2 independent parts, one for each index of `grp`. A program takes and returns all parts, laid end to end along the dimension named above; an argument that names none is the same for every part. Nothing has to cross between parts.
Inputs may be any that keep to these rules, and one draw needn't show every extreme that they name: `basis`: lanczos vectors of earlier iterations, not orthogonal.
All inputs are finite; a program needn't handle non-finite values.
Results may differ from a plain program's by a relative error of at most 0.0008.
Values may be sent and summed in bfloat16 or wider, within the bound.
A program may use at most 192 MiB of HBM per device.

v0:
```python
import jax
import jax.numpy as jnp
from jax import lax
from jax.sharding import PartitionSpec as P


def padded_2(cells, sides, width):
    for axis, dim in sides:
        count = lax.axis_size(axis)
        head = lax.slice_in_dim(cells, 0, width, axis=dim)
        tail = lax.slice_in_dim(cells, cells.shape[dim] - width, cells.shape[dim], axis=dim)
        cells = jnp.concatenate(
            [
                lax.ppermute(tail, axis, [(i, (i + 1) % count) for i in range(count)]),
                cells,
                lax.ppermute(head, axis, [((i + 1) % count, i) for i in range(count)]),
            ],
            axis=dim,
        )
    return cells


def for_sending(shard):

    def short(part):
        return part.astype(jnp.bfloat16) if part.dtype == jnp.float32 else part

    return jax.tree.map(short, shard)


def north(f):
    return jnp.concatenate([f[:, :, 1:], jnp.zeros_like(f[:, :, :1])], axis=2)


def south(f):
    return jnp.concatenate([jnp.zeros_like(f[:, :, :1]), f[:, :, :-1]], axis=2)


def upper(f):
    return jnp.concatenate([f[1:], jnp.zeros_like(f[:1])], axis=0)


def lower(f):
    return jnp.concatenate([jnp.zeros_like(f[:1]), f[:-1]], axis=0)


def make_fields(raw):
    return (
        0.2 * jnp.tanh(raw[0]),
        0.2 * jnp.tanh(raw[1]),
        0.04 + 0.11 * jax.nn.sigmoid(raw[2]),
        0.02 + 0.08 * jax.nn.sigmoid(raw[3]),
    )


def tl_step(state, fields):
    u, v, k, m = fields
    padded = padded_2(state.astype(jnp.bfloat16), (("lon", 1),), 1).astype(state.dtype)
    east = padded[:, 2:]
    west = padded[:, :-2]
    nn = north(state)
    ss = south(state)
    return (
        state
        - 0.5 * u * (east - west)
        - 0.5 * v * (nn - ss)
        + k * (east + west + nn + ss - 4.0 * state)
        + m * (upper(state) + lower(state) - 2.0 * state)
    )


def adjoint_step(state, fields):
    u, v, k, m = fields
    flux_v = v * state
    flux_k = k * state
    flux_m = m * state
    padded = padded_2(for_sending(jnp.stack([u * state, flux_k])), (("lon", 2),), 1)
    east = padded[:, :, 2:]
    west = padded[:, :, :-2]
    return (
        state
        + 0.5 * (east[0] - west[0])
        + 0.5 * (north(flux_v) - south(flux_v))
        + (east[1] + west[1] + north(flux_k) + south(flux_k) - 4.0 * flux_k)
        + (upper(flux_m) + lower(flux_m) - 2.0 * flux_m)
    )


def shards(trajectory, lat_order, basis, weight):
    inverse = jnp.argsort(lat_order)
    steps_count = trajectory.shape[1]
    kept = basis.shape[0]
    total = basis.shape[1] * basis.shape[2] * basis.shape[3] * lax.axis_size("lon")
    stored = []
    received = lax.all_to_all(trajectory, "lon", split_axis=4, concat_axis=0, tiled=True)
    tiles = jnp.transpose(jnp.take(received, inverse, axis=0).astype(jnp.float32), (1, 2, 3, 4, 0))
    stored = [make_fields(tiles[step]) for step in range(steps_count)]
    gram = (
        lax.psum(jnp.einsum("kabc,jabc->kj", basis, basis, precision=lax.Precision.HIGHEST), "lon")
        / total
    )
    state = basis[kept - 1]
    for step in range(steps_count):
        state = tl_step(state, stored[step])
    state = weight[:, None, :] * state
    for step in range(steps_count - 1, -1, -1):
        state = adjoint_step(state, stored[step])
    local_proj = jnp.sum(basis * state[None], axis=(1, 2, 3))
    summed, wsquare = lax.psum((local_proj, jnp.sum(state * state)), "lon")
    projections = summed / total
    resid = state - jnp.tensordot(projections, basis, axes=1, precision=lax.Precision.HIGHEST)
    square = (
        wsquare / total
        - 2.0 * jnp.sum(projections * projections)
        + jnp.dot(
            projections,
            jnp.dot(gram, projections, precision=lax.Precision.HIGHEST),
            precision=lax.Precision.HIGHEST,
        )
    )
    beta = jnp.sqrt(square + 1e-06)
    return (resid / beta, jnp.concatenate([projections, beta[None]]))


def solution(mesh):
    placed = (P(("grp", "lon"), None, None, None, None), P(), P("grp", None, "lon", None), P())
    return jax.shard_map(
        shards,
        mesh=mesh,
        in_specs=placed,
        out_specs=(P("grp", "lon", None), P("grp")),
        check_vma=False,
    )
```

profile of v0, /device:TPU:0, one launch (start us, length us, event | category | flops | bytes accessed | tf_op | source)
XLA Modules:
  0.0 257.7 jit_solution(3718182606194728360)
XLA Ops:
  0.6 10.4 %copy.176 = bf16[40,4,4,8,192]{0,3,2,1,4:T(8,128)(2,1)} copy(bf16[40,4,4,8,192]{4,3,2,1,0:T(8,128)(2,1)} %param.4) | data formatting | bytes 3932160 | tf_op args[0]
  11.1 11.4 %reshape.222 = bf16[16,2,30720]{2,1,0:T(2,128)(2,1)} reshape(bf16[192,4,4,8,40]{4,3,2,1,0:T(8,128)(2,1)} %bitcast.277) | data formatting | bytes 3932160
  22.5 7.5 %all-to-all-start = ((bf16[16,2,30720]{2,1,0:T(2,128)(2,1)}), bf16[16,2,30720]{2,1,0:T(2,128)(2,1)S(1)}, u32[]{:S(2)}, u32[]{:S(2)}) async-start(bf16[16,2,30720]{2,1,0:T(2,128)(2,1)} %reshape.222), calls=%async_computation | async-start | bytes 3932160 | tf_op jit(solution)/shard_map/all_to_all | solution.py:95
  30.0 0.6 copy-done.4
  30.7 0.4 collective-permute-start
  31.1 4.0 %collective-permute-start.1 = (bf16[8,1,640]{2,0,1:T(8,128)(2,1)S(1)}, bf16[8,1,640]{2,0,1:T(8,128)(2,1)S(1)}, u32[]{:S(2)}, u32[]{:S(2)}) collective-permute-start(bf16[8,1,640]{2,0,1:T(8,128)(2,1)S(1)} %get-tuple-element.100), channel_id=1, source_target_pairs={{1,0},{2,1},{3,2},{4,3},{5,4},{6,5},{7,6},{8,7},{9,8},{10,9},{11,1... | collective-permute-start | bytes 30728 | tf_op jit(solution)/shard_map/ppermute | solution.py:16
  35.1 4.4 %sort.17 = (s32[640]{0:T(1024)}, s32[640]{0:T(1024)S(1)}) sort(s32[640]{0:T(1024)S(1)} %copy-done.6, s32[640]{0:T(1024)S(1)} %iota.4), dimensions={0}, to_apply=%region_0.0 | sort | flops 6400 | bytes 10240 | tf_op jit(solution)/shard_map/jit(argsort)/sort | solution.py:90
  39.5 4.4 %convolution_bitcast_fusion = f32[4,4]{1,0:T(4,128)S(1)} fusion(f32[4,8,12,640]{3,1,2,0:T(8,128)S(1)} %copy-done), kind=kOutput, calls=%fused_computation.2 | convolution fusion | flops 11796480 | bytes 983104 | tf_op jit(solution)/shard_map/kabc,jabc->kj/dot_general | solution.py:99
  43.9 0.7 slice_bitcast_fusion.1
  44.7 0.9 fusion.162
  45.5 22.0 %collective-permute-done = bf16[8,1,640]{2,0,1:T(8,128)(2,1)S(1)} collective-permute-done((bf16[8,1,640]{2,0,1:T(8,128)(2,1)S(1)}, bf16[8,1,640]{2,0,1:T(8,128)(2,1)S(1)}, u32[]{:S(2)}, u32[]{:S(2)}) %collective-permute-start) | collective-permute-done | bytes 10272 | tf_op jit(solution)/shard_map/ppermute | solution.py:14
  67.5 0.9 maximum_convert_fusion
  68.4 0.5 all-to-all-done
  68.9 10.7 %reshape.223 = bf16[192,4,4,8,40]{4,3,2,1,0:T(8,128)(2,1)} reshape(bf16[16,2,30720]{2,1,0:T(2,128)(2,1)S(1)} %all-to-all-done) | data formatting | bytes 3932160
  79.6 40.9 %copy.189 = bf16[16,40,4,4,8,12]{5,4,3,2,1,0:T(8,128)(2,1)} copy(bf16[16,40,4,4,8,12]{1,4,3,2,5,0:T(8,128)(2,1)} %bitcast.278) | data formatting | bytes 3932160 | tf_op jit(solution)/shard_map/all_to_all | solution.py:95
  120.5 23.6 %gather_fusion = bf16[640,4,4,8,12]{4,3,2,1,0:T(8,128)(2,1)} fusion(bf16[640,4,4,8,12]{4,3,2,1,0:T(8,128)(2,1)} %bitcast.276, s32[1024]{0:T(1024)S(1)} %pad_clamp_fusion), kind=kCustom, calls=%fused_computation | custom fusion | bytes 3934720 | tf_op jit(solution)/shard_map/jit(_take)/gather | solution.py:96
  144.1 19.6 %copy.180 = bf16[640,4,4,8,12]{0,3,4,2,1:T(8,128)(2,1)S(1)} copy(bf16[640,4,4,8,12]{4,3,2,1,0:T(8,128)(2,1)} %gather_fusion) | data formatting | bytes 3932160 | tf_op jit(solution)/shard_map/jit(_take)/gather | solution.py:96
  163.7 0.3 convert_bitcast_fusion
  164.0 0.6 copy-done.1
  164.6 0.1 copy-done.2
  164.7 0.1 copy-done.3
  164.9 0.4 fusion.142
  165.2 0.8 collective-permute-start.2
  166.0 8.5 %collective-permute-start.3 = (bf16[8,1,640]{2,0,1:T(8,128)(2,1)S(1)}, bf16[8,1,640]{2,0,1:T(8,128)(2,1)S(1)}, u32[]{:S(2)}, u32[]{:S(2)}) collective-permute-start(bf16[8,1,640]{2,0,1:T(8,128)(2,1)S(1)} %get-tuple-element.98), channel_id=1, source_target_pairs={{1,0},{2,1},{3,2},{4,3},{5,4},{6,5},{7,6},{8,7},{9,8},{10,9},{11,1... | collective-permute-start | bytes 30728 | tf_op jit(solution)/shard_map/ppermute | solution.py:16
  174.7 1.1 collective-permute-done.2
  176.0 0.4 fusion.140
  176.4 4.5 %collective-permute-start.5 = (bf16[8,1,640]{2,0,1:T(8,128)(2,1)S(1)}, bf16[8,1,640]{2,0,1:T(8,128)(2,1)S(1)}, u32[]{:S(2)}, u32[]{:S(2)}) collective-permute-start(bf16[8,1,640]{2,0,1:T(8,128)(2,1)S(1)} %get-tuple-element.96), channel_id=1, source_target_pairs={{1,0},{2,1},{3,2},{4,3},{5,4},{6,5},{7,6},{8,7},{9,8},{10,9},{11,1... | collective-permute-start | bytes 30728 | tf_op jit(solution)/shard_map/ppermute | solution.py:16
  181.0 1.1 collective-permute-done.4
  182.3 0.4 fusion.138
  182.7 4.7 %collective-permute-start.7 = (bf16[8,1,640]{2,0,1:T(8,128)(2,1)S(1)}, bf16[8,1,640]{2,0,1:T(8,128)(2,1)S(1)}, u32[]{:S(2)}, u32[]{:S(2)}) collective-permute-start(bf16[8,1,640]{2,0,1:T(8,128)(2,1)S(1)} %get-tuple-element.94), channel_id=1, source_target_pairs={{1,0},{2,1},{3,2},{4,3},{5,4},{6,5},{7,6},{8,7},{9,8},{10,9},{11,1... | collective-permute-start | bytes 30728 | tf_op jit(solution)/shard_map/ppermute | solution.py:16
  187.6 0.9 collective-permute-done.6
  188.5 0.3 collective-permute-done.7
  188.8 0.4 fusion.95
  189.2 0.2 convert_bitcast_fusion.4
  189.4 4.5 %collective-permute-start.8 = (bf16[2,8,1,640]{3,1,2,0:T(8,128)(2,1)S(1)}, bf16[2,8,1,640]{3,1,2,0:T(8,128)(2,1)S(1)}, u32[]{:S(2)}, u32[]{:S(2)}) collective-permute-start(bf16[2,8,1,640]{3,1,2,0:T(8,128)(2,1)S(1)} %get-tuple-element.73), channel_id=1, source_target_pairs={{1,0},{2,1},{3,2},{4,3},{5,4},{6,5},{7,6},{8,7},{9,8},{10,9},{11,1... | collective-permute-start | bytes 61448 | tf_op jit(solution)/shard_map/ppermute | solution.py:16
  193.9 0.2 fusion.153
  194.1 1.2 collective-permute-done.8
  195.4 4.4 %collective-permute-done.9 = bf16[2,8,1,640]{3,1,2,0:T(8,128)(2,1)S(1)} collective-permute-done((bf16[2,8,1,640]{3,1,2,0:T(8,128)(2,1)S(1)}, bf16[2,8,1,640]{3,1,2,0:T(8,128)(2,1)S(1)}, u32[]{:S(2)}, u32[]{:S(2)}) %collective-permute-start.9) | collective-permute-done | bytes 20512 | tf_op jit(solution)/shard_map/ppermute | solution.py:14
  199.8 0.4 fusion.96
  200.1 0.2 convert_bitcast_fusion.3
  200.4 0.5 collective-permute-start.11
  201.0 0.1 fusion.151
  201.2 0.7 collective-permute-done.10
  201.9 4.5 %collective-permute-done.11 = bf16[2,8,1,640]{3,1,2,0:T(8,128)(2,1)S(1)} collective-permute-done((bf16[2,8,1,640]{3,1,2,0:T(8,128)(2,1)S(1)}, bf16[2,8,1,640]{3,1,2,0:T(8,128)(2,1)S(1)}, u32[]{:S(2)}, u32[]{:S(2)}) %collective-permute-start.11) | collective-permute-done | bytes 20512 | tf_op jit(solution)/shard_map/ppermute | solution.py:14
  206.4 0.4 fusion.97
  206.8 0.2 convert_bitcast_fusion.2
  207.0 0.5 collective-permute-start.13
  207.6 0.1 fusion.148
  207.8 0.7 collective-permute-done.12
  208.5 4.5 %collective-permute-done.13 = bf16[2,8,1,640]{3,1,2,0:T(8,128)(2,1)S(1)} collective-permute-done((bf16[2,8,1,640]{3,1,2,0:T(8,128)(2,1)S(1)}, bf16[2,8,1,640]{3,1,2,0:T(8,128)(2,1)S(1)}, u32[]{:S(2)}, u32[]{:S(2)}) %collective-permute-start.13) | collective-permute-done | bytes 20512 | tf_op jit(solution)/shard_map/ppermute | solution.py:14
  213.0 0.4 fusion.98
  213.4 0.2 convert_bitcast_fusion.1
  213.6 0.5 collective-permute-start.15
  214.2 0.1 fusion.145
  214.4 0.7 collective-permute-done.14
  215.1 4.5 %collective-permute-done.15 = bf16[2,8,1,640]{3,1,2,0:T(8,128)(2,1)S(1)} collective-permute-done((bf16[2,8,1,640]{3,1,2,0:T(8,128)(2,1)S(1)}, bf16[2,8,1,640]{3,1,2,0:T(8,128)(2,1)S(1)}, u32[]{:S(2)}, u32[]{:S(2)}) %collective-permute-start.15) | collective-permute-done | bytes 20512 | tf_op jit(solution)/shard_map/ppermute | solution.py:14
  219.6 0.9 multiply_reduce_fusion.1
  220.5 0.2 multiply_reduce_fusion
  220.7 30.1 %all-reduce.40 = (f32[4]{0:T(128)S(1)}, f32[]{:T(128)}, f32[4,4]{1,0:T(4,128)S(1)}) all-reduce(f32[4]{0:T(128)S(1)} %multiply_reduce_fusion, f32[]{:T(128)} %get-tuple-element.13, f32[4,4]{1,0:T(4,128)S(1)} %convolution_bitcast_fusion), channel_id=1, replica_groups=mesh['grp'=2,'lon'=16] {'lon'}, use_global_device_ids=true, to_apply=%region_2.3 | all-reduce | flops 21 | bytes 168 | tf_op jit(solution)/shard_map/psum | solution.py:109
  250.8 0.6 broadcast_multiply_fusion
  251.4 2.2 fusion.1
  253.7 0.8 fusion.4
  256.4 0.7 fusion.73
  257.1 0.6 pad_maximum_fusion.24
  (49 shorter events, 1.6 us)
Async XLA Ops:
  22.5 7.5 %copy-start = (f32[4,8,12,640]{3,1,2,0:T(8,128)S(1)}, f32[4,8,12,640]{3,1,2,0:T(8,128)}, u32[]{:S(2)}) copy-start(f32[4,8,12,640]{3,1,2,0:T(8,128)} %param.6) | copy-start | bytes 2949124
  22.5 12.7 %copy-start.6 = (s32[640]{0:T(1024)S(1)}, s32[640]{0:T(1024)}, u32[]{:S(2)}) copy-start(s32[640]{0:T(1024)} %param.5) | copy-start | bytes 7684
  22.5 46.5 %all-to-all-start = ((bf16[16,2,30720]{2,1,0:T(2,128)(2,1)}), bf16[16,2,30720]{2,1,0:T(2,128)(2,1)S(1)}, u32[]{:S(2)}, u32[]{:S(2)}) async-start(bf16[16,2,30720]{2,1,0:T(2,128)(2,1)} %reshape.222), calls=%async_computation | async-start | bytes 3932160 | tf_op jit(solution)/shard_map/all_to_all | solution.py:95
  30.0 0.6 copy-start.4
  30.7 36.8 %collective-permute-start = (bf16[8,1,640]{2,0,1:T(8,128)(2,1)S(1)}, bf16[8,1,640]{2,0,1:T(8,128)(2,1)S(1)}, u32[]{:S(2)}, u32[]{:S(2)}) collective-permute-start(bf16[8,1,640]{2,0,1:T(8,128)(2,1)S(1)} %get-tuple-element.99), channel_id=1, source_target_pairs={{0,1},{1,2},{2,3},{3,4},{4,5},{5,6},{6,7},{7,8},{8,9},{9,10},{10,1... | collective-permute-start | bytes 30728 | tf_op jit(solution)/shard_map/ppermute | solution.py:14
  31.1 36.4 %collective-permute-start.1 = (bf16[8,1,640]{2,0,1:T(8,128)(2,1)S(1)}, bf16[8,1,640]{2,0,1:T(8,128)(2,1)S(1)}, u32[]{:S(2)}, u32[]{:S(2)}) collective-permute-start(bf16[8,1,640]{2,0,1:T(8,128)(2,1)S(1)} %get-tuple-element.100), channel_id=1, source_target_pairs={{1,0},{2,1},{3,2},{4,3},{5,4},{6,5},{7,6},{8,7},{9,8},{10,9},{11,1... | collective-permute-start | bytes 30728 | tf_op jit(solution)/shard_map/ppermute | solution.py:16
  163.7 0.9 copy-start.1
  163.7 1.1 copy-start.2
  163.7 1.2 copy-start.3
  165.2 10.6 %collective-permute-start.2 = (bf16[8,1,640]{2,0,1:T(8,128)(2,1)S(1)}, bf16[8,1,640]{2,0,1:T(8,128)(2,1)S(1)}, u32[]{:S(2)}, u32[]{:S(2)}) collective-permute-start(bf16[8,1,640]{2,0,1:T(8,128)(2,1)S(1)} %get-tuple-element.97), channel_id=1, source_target_pairs={{0,1},{1,2},{2,3},{3,4},{4,5},{5,6},{6,7},{7,8},{8,9},{9,10},{10,1... | collective-permute-start | bytes 30728 | tf_op jit(solution)/shard_map/ppermute | solution.py:14
  166.0 9.9 %collective-permute-start.3 = (bf16[8,1,640]{2,0,1:T(8,128)(2,1)S(1)}, bf16[8,1,640]{2,0,1:T(8,128)(2,1)S(1)}, u32[]{:S(2)}, u32[]{:S(2)}) collective-permute-start(bf16[8,1,640]{2,0,1:T(8,128)(2,1)S(1)} %get-tuple-element.98), channel_id=1, source_target_pairs={{1,0},{2,1},{3,2},{4,3},{5,4},{6,5},{7,6},{8,7},{9,8},{10,9},{11,1... | collective-permute-start | bytes 30728 | tf_op jit(solution)/shard_map/ppermute | solution.py:16
  176.3 5.8 %collective-permute-start.4 = (bf16[8,1,640]{2,0,1:T(8,128)(2,1)S(1)}, bf16[8,1,640]{2,0,1:T(8,128)(2,1)S(1)}, u32[]{:S(2)}, u32[]{:S(2)}) collective-permute-start(bf16[8,1,640]{2,0,1:T(8,128)(2,1)S(1)} %get-tuple-element.95), channel_id=1, source_target_pairs={{0,1},{1,2},{2,3},{3,4},{4,5},{5,6},{6,7},{7,8},{8,9},{9,10},{10,1... | collective-permute-start | bytes 30728 | tf_op jit(solution)/shard_map/ppermute | solution.py:14
  176.4 5.8 %collective-permute-start.5 = (bf16[8,1,640]{2,0,1:T(8,128)(2,1)S(1)}, bf16[8,1,640]{2,0,1:T(8,128)(2,1)S(1)}, u32[]{:S(2)}, u32[]{:S(2)}) collective-permute-start(bf16[8,1,640]{2,0,1:T(8,128)(2,1)S(1)} %get-tuple-element.96), channel_id=1, source_target_pairs={{1,0},{2,1},{3,2},{4,3},{5,4},{6,5},{7,6},{8,7},{9,8},{10,9},{11,1... | collective-permute-start | bytes 30728 | tf_op jit(solution)/shard_map/ppermute | solution.py:16
  180.9 8.0 %copy-start.5 = (f32[8,640]{1,0:T(8,128)S(1)}, f32[8,640]{1,0:T(8,128)}, u32[]{:S(2)}) copy-start(f32[8,640]{1,0:T(8,128)} %param.7) | copy-start | bytes 61444
  182.7 5.9 %collective-permute-start.6 = (bf16[8,1,640]{2,0,1:T(8,128)(2,1)S(1)}, bf16[8,1,640]{2,0,1:T(8,128)(2,1)S(1)}, u32[]{:S(2)}, u32[]{:S(2)}) collective-permute-start(bf16[8,1,640]{2,0,1:T(8,128)(2,1)S(1)} %get-tuple-element.93), channel_id=1, source_target_pairs={{0,1},{1,2},{2,3},{3,4},{4,5},{5,6},{6,7},{7,8},{8,9},{9,10},{10,1... | collective-permute-start | bytes 30728 | tf_op jit(solution)/shard_map/ppermute | solution.py:14
  182.7 6.1 %collective-permute-start.7 = (bf16[8,1,640]{2,0,1:T(8,128)(2,1)S(1)}, bf16[8,1,640]{2,0,1:T(8,128)(2,1)S(1)}, u32[]{:S(2)}, u32[]{:S(2)}) collective-permute-start(bf16[8,1,640]{2,0,1:T(8,128)(2,1)S(1)} %get-tuple-element.94), channel_id=1, source_target_pairs={{1,0},{2,1},{3,2},{4,3},{5,4},{6,5},{7,6},{8,7},{9,8},{10,9},{11,1... | collective-permute-start | bytes 30728 | tf_op jit(solution)/shard_map/ppermute | solution.py:16
  189.4 5.9 %collective-permute-start.8 = (bf16[2,8,1,640]{3,1,2,0:T(8,128)(2,1)S(1)}, bf16[2,8,1,640]{3,1,2,0:T(8,128)(2,1)S(1)}, u32[]{:S(2)}, u32[]{:S(2)}) collective-permute-start(bf16[2,8,1,640]{3,1,2,0:T(8,128)(2,1)S(1)} %get-tuple-element.73), channel_id=1, source_target_pairs={{1,0},{2,1},{3,2},{4,3},{5,4},{6,5},{7,6},{8,7},{9,8},{10,9},{11,1... | collective-permute-start | bytes 61448 | tf_op jit(solution)/shard_map/ppermute | solution.py:16
  193.9 5.9 %collective-permute-start.9 = (bf16[2,8,1,640]{3,1,2,0:T(8,128)(2,1)S(1)}, bf16[2,8,1,640]{3,1,2,0:T(8,128)(2,1)S(1)}, u32[]{:S(2)}, u32[]{:S(2)}) collective-permute-start(bf16[2,8,1,640]{3,1,2,0:T(8,128)(2,1)S(1)} %get-tuple-element.74), channel_id=1, source_target_pairs={{0,1},{1,2},{2,3},{3,4},{4,5},{5,6},{6,7},{7,8},{8,9},{9,10},{10,1... | collective-permute-start | bytes 61448 | tf_op jit(solution)/shard_map/ppermute | solution.py:14
  200.3 1.5 collective-permute-start.10
  200.4 6.0 %collective-permute-start.11 = (bf16[2,8,1,640]{3,1,2,0:T(8,128)(2,1)S(1)}, bf16[2,8,1,640]{3,1,2,0:T(8,128)(2,1)S(1)}, u32[]{:S(2)}, u32[]{:S(2)}) collective-permute-start(bf16[2,8,1,640]{3,1,2,0:T(8,128)(2,1)S(1)} %get-tuple-element.66), channel_id=1, source_target_pairs={{0,1},{1,2},{2,3},{3,4},{4,5},{5,6},{6,7},{7,8},{8,9},{9,10},{10,1... | collective-permute-start | bytes 61448 | tf_op jit(solution)/shard_map/ppermute | solution.py:14
  207.0 1.5 collective-permute-start.12
  207.0 6.0 %collective-permute-start.13 = (bf16[2,8,1,640]{3,1,2,0:T(8,128)(2,1)S(1)}, bf16[2,8,1,640]{3,1,2,0:T(8,128)(2,1)S(1)}, u32[]{:S(2)}, u32[]{:S(2)}) collective-permute-start(bf16[2,8,1,640]{3,1,2,0:T(8,128)(2,1)S(1)} %get-tuple-element.58), channel_id=1, source_target_pairs={{0,1},{1,2},{2,3},{3,4},{4,5},{5,6},{6,7},{7,8},{8,9},{9,10},{10,1... | collective-permute-start | bytes 61448 | tf_op jit(solution)/shard_map/ppermute | solution.py:14
  213.6 1.5 collective-permute-start.14
  213.6 6.0 %collective-permute-start.15 = (bf16[2,8,1,640]{3,1,2,0:T(8,128)(2,1)S(1)}, bf16[2,8,1,640]{3,1,2,0:T(8,128)(2,1)S(1)}, u32[]{:S(2)}, u32[]{:S(2)}) collective-permute-start(bf16[2,8,1,640]{3,1,2,0:T(8,128)(2,1)S(1)} %get-tuple-element.50), channel_id=1, source_target_pairs={{0,1},{1,2},{2,3},{3,4},{4,5},{5,6},{6,7},{7,8},{8,9},{9,10},{10,1... | collective-permute-start | bytes 61448 | tf_op jit(solution)/shard_map/ppermute | solution.py:14
where the time goes:
time: 259 us; the launch traced here: 258 us
  local copies, waits for them, and re-layouts  121 us (47%)
  waiting for transfers between devices  47.3 us (18%)
  starting transfers between devices  36.7 us (14%)
  blocking collectives  30.1 us (12%)
  other arithmetic  12 us (5%)
  matrix products  7.39 us (3%)
  between operations  3 us (1%)
    gather x2, local copies, waits for them, and re-layouts, shards(): jnp.take(received, inverse, axis=0).astype(jnp.float32)  43.1 us
    ppermute x8, waiting for transfers between devices, padded_2(): lax.ppermute(tail, axis, [(i, (i + 1) % count) for i in range(count)])  43.1 us
    all_to_all x1, local copies, waits for them, and re-layouts, shards(): lax.all_to_all(trajectory, 'lon', split_axis=4, concat_axis=0, tiled=True)  40.9 us
    unnamed x17, local copies, waits for them, and re-layouts  34 us
    psum x1, blocking collectives, shards(): summed, wsquare = lax.psum((local_proj, jnp.sum(state * state)), 'lon')  30.1 us
    ppermute x8, starting transfers between devices, padded_2(): lax.ppermute(head, axis, [((i + 1) % count, i) for i in range(count)])  26.3 us
    all_to_all x1, starting transfers between devices, shards(): lax.all_to_all(trajectory, 'lon', split_axis=4, concat_axis=0, tiled=True)  7.52 us
  transfers between devices with their start and end apart: 17, of which 16 were waited for; matrix products, arithmetic and copies ran while one was open for 5% of the time, Pallas kernels for 0%

commit v1 on v0

v1 whole, which is shorter than its diff:
```python
import functools

import jax
import jax.numpy as jnp
from jax import lax
from jax.experimental import pallas as pl
from jax.experimental.pallas import tpu as pltpu
from jax.sharding import PartitionSpec as P

BF16 = jnp.bfloat16
F32 = jnp.float32
VMEM = pl.BlockSpec(memory_space=pltpu.VMEM)
MIB = 1024 * 1024


def pairs(kept):
    return [(a, b) for a in range(kept) for b in range(a, kept)]


def pack_kernel(rows, t_ref, out_ref, wide):
    lons = t_ref.shape[2]
    eye = (
        lax.broadcasted_iota(jnp.int32, (lons, lons), 0)
        == lax.broadcasted_iota(jnp.int32, (lons, lons), 1)
    ).astype(F32).astype(BF16)
    for r in range(rows):
        turned = lax.dot_general(
            eye, t_ref[r], (((1,), (1,)), ((), ())), preferred_element_type=F32
        )
        wide[pl.ds(r, lons, stride=rows), :] = turned
    out_ref[...] = wide[...].astype(BF16)


def row_sum(cells):
    total = jnp.sum(jnp.sum(cells, axis=0), axis=0, keepdims=True)
    return sum(total[:, at : at + 128] for at in range(0, total.shape[1], 128))


def prep_kernel(lat_ref, basis_ref, perm_ref, gram_ref):
    lats = perm_ref.shape[0]
    kept = basis_ref.shape[0]
    perm_ref[...] = (
        (lat_ref[...] == lax.broadcasted_iota(jnp.int32, (lats, lats), 1))
        .astype(F32)
        .astype(BF16)
    )
    gram_ref[...] = jnp.zeros_like(gram_ref)
    for at, (a, b) in enumerate(pairs(kept)):
        gram_ref[kept + 1 + at : kept + 2 + at, :] = row_sum(basis_ref[a] * basis_ref[b])


def main_kernel(
    count, rows, cells, recv_ref, perm_ref, basis_ref, weight_ref, gram_ref,
    out_ref, coef_ref,
    wide, coefs, state, halo, edge, gathered,
    halo_send, halo_recv, sum_send, sum_recv,
):
    kept, tile, levels, lats = basis_ref.shape
    steps = coefs.shape[0]
    me = lax.axis_index("lon")
    west = lax.rem(me + count - 1, count)
    east = lax.rem(me + 1, count)
    barrier = pltpu.get_barrier_semaphore()

    @pl.loop(1, count)
    def _(d):
        pl.semaphore_signal(
            barrier, inc=1, device_id={"lon": lax.rem(me + d, count)},
            device_id_type=pl.DeviceIdType.MESH,
        )

    wide[...] = recv_ref[...].astype(F32)
    level = lax.broadcasted_iota(jnp.int32, (levels, lats), 0)
    lat = lax.broadcasted_iota(jnp.int32, (levels, lats), 1)
    up = (level < levels - 1).astype(F32)
    down = (level > 0).astype(F32)
    not_north = (lat < lats - 1).astype(F32)
    not_south = (lat > 0).astype(F32)

    def fields(i, _):
        block = wide[:, pl.ds(pl.multiple_of(i * rows, 8), rows), :]
        block = block.reshape(lats, block.shape[2]).astype(BF16)
        raw = lax.dot_general(
            block, perm_ref[...], (((0,), (0,)), ((), ())), preferred_element_type=F32
        ).reshape(steps, 4, levels, lats)
        u = 0.1 * jnp.tanh(raw[:, 0])
        v = 0.1 * jnp.tanh(raw[:, 1])
        k = 0.095 + 0.055 * jnp.tanh(0.5 * raw[:, 2])
        m = 0.06 + 0.04 * jnp.tanh(0.5 * raw[:, 3])
        coefs[:, 0, i] = 1.0 - 4.0 * k - 2.0 * m
        coefs[:, 1, i] = k - u
        coefs[:, 2, i] = k + u
        coefs[:, 3, i] = (k - v) * not_north
        coefs[:, 4, i] = (k + v) * not_south
        coefs[:, 5, i] = m
        return 0

    def copies(slot):
        return [
            pltpu.make_async_remote_copy(
                src_ref=edge.at[slot, side],
                dst_ref=halo.at[slot, side],
                send_sem=halo_send.at[slot, side],
                recv_sem=halo_recv.at[slot, side],
                device_id={"lon": peer},
                device_id_type=pl.DeviceIdType.MESH,
            )
            for side, peer in ((0, west), (1, east))
        ]

    def send(slot, first, last):
        edge[slot, 0] = first
        edge[slot, 1] = last
        for copy in copies(slot):
            copy.start()

    def receive(slot):
        for copy in copies(slot):
            copy.wait_recv()
        return halo[slot, 0][None], halo[slot, 1][None]

    def roll(x, by, axis):
        shape = x.shape
        if axis == 2:
            return pltpu.roll(x.reshape(-1, lats), by % lats, 1).reshape(shape)
        return pltpu.roll(x, by % levels, 1)

    def forward(s, lo, hi, x, xe, xw):
        c = lambda at: coefs[s, at, lo:hi]
        return (
            c(0) * x
            + c(1) * xe
            + c(2) * xw
            + c(3) * roll(x, -1, 2)
            + c(4) * roll(x, 1, 2)
            + c(5) * (up * roll(x, -1, 1) + down * roll(x, 1, 1))
        )

    def adjoint(s, lo, hi, y, fe, fw):
        c = lambda at: coefs[s, at, lo:hi]
        d = c(5) * y
        return (
            c(0) * y
            + fe
            + fw
            + roll(c(4) * y, -1, 2)
            + roll(c(3) * y, 1, 2)
            + roll(down * d, -1, 1)
            + roll(up * d, 1, 1)
        )

    half = tile // 2
    lax.fori_loop(0, half, fields, 0)
    pl.semaphore_wait(barrier, count - 1)
    state[0] = basis_ref[kept - 1]
    send(0, state[0, 0], state[0, tile - 1])
    lax.fori_loop(half, tile, fields, 0)

    for t in range(2 * steps):
        now, new = t % 2, (t + 1) % 2
        if t < steps:
            s = t
            inside = forward(
                s, 1, tile - 1, state[now, 1 : tile - 1],
                state[now, 2:tile], state[now, 0 : tile - 2],
            )
            he, hw = receive(t)
            first = forward(s, 0, 1, state[now, 0:1], state[now, 1:2], hw)
            last = forward(
                s, tile - 1, tile, state[now, tile - 1 : tile], he,
                state[now, tile - 2 : tile - 1],
            )
            if t == steps - 1:
                inside = weight_ref[...] * inside
                first = weight_ref[...] * first
                last = weight_ref[...] * last
        else:
            s = 2 * steps - 1 - t
            inside = adjoint(
                s, 1, tile - 1, state[now, 1 : tile - 1],
                coefs[s, 2, 2:tile] * state[now, 2:tile],
                coefs[s, 1, 0 : tile - 2] * state[now, 0 : tile - 2],
            )
            he, hw = receive(t)
            first = adjoint(
                s, 0, 1, state[now, 0:1], coefs[s, 2, 1:2] * state[now, 1:2], hw
            )
            last = adjoint(
                s, tile - 1, tile, state[now, tile - 1 : tile], he,
                coefs[s, 1, tile - 2 : tile - 1] * state[now, tile - 2 : tile - 1],
            )
        if t < steps - 1:
            send(t + 1, first[0], last[0])
        elif t < 2 * steps - 1:
            s = 2 * steps - 2 - t
            send(t + 1, coefs[s, 2, 0] * first[0], coefs[s, 1, tile - 1] * last[0])
        state[new, 0:1] = first
        state[new, tile - 1 : tile] = last
        state[new, 1 : tile - 1] = inside

    w = state[0]
    own = [row_sum(basis_ref[k] * w) for k in range(kept)] + [row_sum(w * w)]
    gathered[me] = gram_ref[...]
    for k in range(kept + 1):
        gathered[me, k : k + 1, :] = own[k]

    def share(d):
        return pltpu.make_async_remote_copy(
            src_ref=gathered.at[me],
            dst_ref=gathered.at[me],
            send_sem=sum_send.at[d],
            recv_sem=sum_recv.at[me],
            device_id={"lon": lax.rem(me + d, count)},
            device_id_type=pl.DeviceIdType.MESH,
        )

    @pl.loop(1, count)
    def _(d):
        share(d).start()

    @pl.loop(1, count)
    def _(d):
        source = lax.rem(me + d, count)
        pltpu.make_async_remote_copy(
            src_ref=gathered.at[source],
            dst_ref=gathered.at[source],
            send_sem=sum_send.at[d],
            recv_sem=sum_recv.at[source],
            device_id={"lon": source},
            device_id_type=pl.DeviceIdType.MESH,
        ).wait_recv()

    total = jnp.sum(jnp.sum(gathered[...], axis=0), axis=1, keepdims=True) / cells
    c = [total[k : k + 1] for k in range(kept)]
    square = total[kept : kept + 1] - 2.0 * sum(x * x for x in c)
    for at, (a, b) in enumerate(pairs(kept)):
        g = total[kept + 1 + at : kept + 2 + at]
        square = square + (1.0 if a == b else 2.0) * c[a] * c[b] * g
    beta = jnp.sqrt(square + 1e-06)
    for k in range(kept):
        coef_ref[k : k + 1, :] = jnp.broadcast_to(c[k], (1, 128))
    coef_ref[kept : kept + 1, :] = jnp.broadcast_to(beta, (1, 128))
    coef_ref[kept + 1 :, :] = jnp.zeros((8 - kept - 1, 128), F32)
    scale = jnp.broadcast_to(1.0 / beta, (levels, lats))
    full = [jnp.broadcast_to(x, (levels, lats)) for x in c]
    for i in range(tile):
        r = state[0, i]
        for k in range(kept):
            r = r - full[k] * basis_ref[k, i]
        out_ref[i] = r * scale

    for t in range(2 * steps):
        for copy in copies(t):
            copy.wait_send()

    @pl.loop(1, count)
    def _(d):
        share(d).wait_send()


def shards(trajectory, lat_order, basis, weight):
    rows, steps, states, levels, lons = trajectory.shape
    kept, _, tile, lats = basis.shape
    count = lax.axis_size("lon")
    lanes = steps * states * levels
    cells = float(levels * lons * lats)
    flat = trajectory.reshape(rows, lanes, lons)
    if rows % 8 == 0:
        packed = pl.pallas_call(
            functools.partial(pack_kernel, rows),
            out_shape=jax.ShapeDtypeStruct((lons * rows, lanes), BF16),
            in_specs=[VMEM],
            out_specs=VMEM,
            scratch_shapes=[pltpu.VMEM((lons * rows, lanes), F32)],
            compiler_params=pltpu.CompilerParams(vmem_limit_bytes=24 * MIB),
            name="pack",
        )(flat)
    else:
        packed = jnp.transpose(flat, (2, 0, 1))
    received = lax.all_to_all(
        packed.reshape(count, tile * rows, lanes), "lon", split_axis=0, concat_axis=0, tiled=True
    )
    if rows % 8:
        received = jnp.transpose(received.reshape(count, tile, rows, lanes), (1, 0, 2, 3))
        received = received.reshape(1, tile * lats, lanes)
        rows = lats
    turned = jnp.transpose(basis, (0, 2, 1, 3))
    perm, gram = pl.pallas_call(
        prep_kernel,
        out_shape=(
            jax.ShapeDtypeStruct((lats, lats), BF16),
            jax.ShapeDtypeStruct((16, 128), F32),
        ),
        in_specs=[VMEM] * 2,
        out_specs=(VMEM, VMEM),
        cost_estimate=pl.CostEstimate(
            flops=20_000_000, bytes_accessed=4_000_000, transcendentals=0
        ),
        compiler_params=pltpu.CompilerParams(vmem_limit_bytes=16 * MIB),
        name="prepare",
    )(lat_order[:, None], turned)
    slots = 2 * steps
    out, coef = pl.pallas_call(
        functools.partial(main_kernel, count, rows, cells),
        out_shape=(
            jax.ShapeDtypeStruct((tile, levels, lats), F32),
            jax.ShapeDtypeStruct((8, 128), F32),
        ),
        in_specs=[VMEM] * 5,
        out_specs=(VMEM, VMEM),
        scratch_shapes=[
            pltpu.VMEM(received.shape, F32),
            pltpu.VMEM((steps, 6, tile, levels, lats), F32),
            pltpu.VMEM((2, tile, levels, lats), F32),
            pltpu.VMEM((slots, 2, levels, lats), F32),
            pltpu.VMEM((slots, 2, levels, lats), F32),
            pltpu.VMEM((count, 16, 128), F32),
            pltpu.SemaphoreType.DMA((slots, 2)),
            pltpu.SemaphoreType.DMA((slots, 2)),
            pltpu.SemaphoreType.DMA((count,)),
            pltpu.SemaphoreType.DMA((count,)),
        ],
        compiler_params=pltpu.CompilerParams(
            collective_id=0, has_side_effects=True, vmem_limit_bytes=40 * MIB
        ),
        name="iterate",
    )(received, perm, turned, weight, gram)
    return jnp.transpose(out, (1, 0, 2)), coef[: kept + 1, 0]


def solution(mesh):
    placed = (P(("grp", "lon"), None, None, None, None), P(), P("grp", None, "lon", None), P())
    return jax.shard_map(
        shards,
        mesh=mesh,
        in_specs=placed,
        out_specs=(P("grp", "lon", None), P("grp")),
        check_vma=False,
    )
```

time: 259 us -> 98.4 us (0.38)
  local copies, waits for them, and re-layouts: 121 us -> 6.57 us
  Pallas kernels: 0 us -> 46.1 us
  blocking collectives: 30.1 us -> 0 us
  starting transfers between devices: 36.7 us -> 7.52 us
  other arithmetic: 12 us -> 0 us
  waiting for transfers between devices: 47.3 us -> 37.3 us
  matrix products: 7.39 us -> 0 us
    ppermute x16 -> x0, waiting for transfers between devices: 46.8 us -> none  [the longest x8 43.1 us: padded_2(): lax.ppermute(tail, axis, [(i, (i + 1) % count) for i in range(count)])]
    pallas_call x0 -> x3, Pallas kernels: none -> 46.1 us  [the longest x1 44.3 us: shards(): pl.pallas_call(functools.partial(main_kernel, count, rows, cells), out_sh...]
    gather x2 -> x0, local copies, waits for them, and re-layouts: 43.1 us -> none  [shards(): jnp.take(received, inverse, axis=0).astype(jnp.float32)]
    all_to_all x1 -> x0, local copies, waits for them, and re-layouts: 40.9 us -> none  [shards(): lax.all_to_all(trajectory, 'lon', split_axis=4, concat_axis=0, tiled=True)]
    all_to_all x1, waiting for transfers between devices: 0.49 us -> 37.3 us  [shards(): lax.all_to_all(packed.reshape(count, tile * rows, lanes), 'lon', split_ax...]
    psum x1 -> x0, blocking collectives: 30.1 us -> none  [shards(): summed, wsquare = lax.psum((local_proj, jnp.sum(state * state)), 'lon')]
    ppermute x16 -> x0, starting transfers between devices: 29.2 us -> none  [the longest x8 26.3 us: padded_2(): lax.ppermute(head, axis, [((i + 1) % count, i) for i in range(count)])]
    unnamed x17 -> x15, local copies, waits for them, and re-layouts: 34 us -> 5.8 us
  transfers between devices with their start and end apart: 17 -> 1, of which waited for: 16 -> 1; matrix products, arithmetic and copies ran while one was open for 5% -> 0% of each run, Pallas kernels for 0% -> 0%
where the time goes in v1:
time: 98.4 us; the launch traced here: 98.2 us
  Pallas kernels  46.1 us (47%)
  waiting for transfers between devices  37.3 us (38%)
  starting transfers between devices  7.52 us (8%)
  local copies, waits for them, and re-layouts  6.57 us (7%)
    pallas_call x1, Pallas kernels, shards(): pl.pallas_call(functools.partial(main_kernel, count, rows, cells), out_sh...  44.3 us
    all_to_all x1, waiting for transfers between devices, shards(): lax.all_to_all(packed.reshape(count, tile * rows, lanes), 'lon', split_ax...  37.3 us
    all_to_all x1, starting transfers between devices, shards(): lax.all_to_all(packed.reshape(count, tile * rows, lanes), 'lon', split_ax...  7.52 us
    unnamed x15, local copies, waits for them, and re-layouts  5.8 us
  transfers between devices with their start and end apart: 1, of which 1 were waited for; matrix products, arithmetic and copies ran while one was open for 0% of the time, Pallas kernels for 0%

profile of v1, /device:TPU:0, one launch (start us, length us, event | category | flops | bytes accessed | tf_op | source)
XLA Modules:
  0.0 98.2 jit_solution(12430829774583004939)
XLA Ops:
  0.6 0.0 copy-start.2
  0.6 1.7 %copy-done.2 = bf16[40,4,4,8,192]{4,3,2,1,0:T(8,128)(2,1)S(1)} copy-done((bf16[40,4,4,8,192]{4,3,2,1,0:T(8,128)(2,1)S(1)}, bf16[40,4,4,8,192]{4,3,2,1,0:T(8,128)(2,1)}, u32[]{:S(2)}) %copy-start.2) | copy-done | bytes 1966104
  2.4 1.3 %pack.1 = bf16[7680,128]{1,0:T(8,128)(2,1)S(1)} custom-call(bf16[40,128,192]{2,1,0:T(8,128)(2,1)S(1)} %bitcast.7), custom_call_target="tpu_custom_call" | custom-call | tf_op jit(solution)/shard_map/pack/pallas_call | solution.py:269
  3.7 0.0 copy-start
  3.7 1.3 %copy-done = bf16[7680,128]{1,0:T(8,128)(2,1)} copy-done((bf16[7680,128]{1,0:T(8,128)(2,1)}, bf16[7680,128]{1,0:T(8,128)(2,1)S(1)}, u32[]{:S(2)}) %copy-start) | copy-done | bytes 1966104
  5.0 0.0 copy-start.6
  5.0 0.0 copy-start.1
  5.0 0.0 copy-start.5
  5.0 7.5 %all-to-all-start = ((bf16[16,480,128]{2,1,0:T(8,128)(2,1)}), bf16[16,480,128]{2,1,0:T(8,128)(2,1)S(1)}, u32[]{:S(2)}, u32[]{:S(2)}) async-start(bf16[16,480,128]{2,1,0:T(8,128)(2,1)} %bitcast.4), calls=%async_computation | async-start | bytes 3932160 | tf_op jit(solution)/shard_map/all_to_all | solution.py:280
  12.5 0.0 copy-done.6
  12.5 0.1 broadcast_in_dim.4.lat_ref
  12.7 0.0 copy-done.1
  12.7 0.4 prepare.1
  13.1 0.0 copy-start.3
  13.1 0.9 copy-done.3
  14.0 37.3 %all-to-all-done.recv_ref = bf16[16,480,128]{2,1,0:T(8,128)(2,1)S(1)} async-done(((bf16[16,480,128]{2,1,0:T(8,128)(2,1)}), bf16[16,480,128]{2,1,0:T(8,128)(2,1)S(1)}, u32[]{:S(2)}, u32[]{:S(2)}) %all-to-all-start) | async-done | bytes 1966112 | tf_op jit(solution)/shard_map/all_to_all | solution.py:280
  51.3 0.0 copy-done.5
  51.3 0.0 copy-start.4
  51.4 1.1 %copy-done.4 = bf16[640,640]{1,0:T(8,128)(2,1)S(1)} copy-done((bf16[640,640]{1,0:T(8,128)(2,1)S(1)}, bf16[640,640]{1,0:T(8,128)(2,1)}, u32[]{:S(2)}) %copy-start.4) | copy-done | bytes 819224
  52.5 44.3 %iterate.1 = (f32[12,8,640]{2,1,0:T(8,128)S(1)}, f32[8,128]{1,0:T(8,128)S(1)}) custom-call(bf16[16,480,128]{2,1,0:T(8,128)(2,1)S(1)} %all-to-all-done.recv_ref, bf16[640,640]{1,0:T(8,128)(2,1)S(1)} %copy-done.4, f32[4,12,8,640]{3,2,1,0:T(8,128)S(1)} %bitcast.6, f32[8,640]{1,0:T(8,128)S(1)} %copy-done.5, f32[16,128]{1,0:T(8,128)S(1)} %get-tuple-element.7.gram_ref), custom_call_target="tpu_custom_call" | custom-call | tf_op jit(solution)/shard_map/iterate/pallas_call | solution.py:303
  96.8 0.6 slice_reduce_fusion
  97.5 0.7 copy.8
Async XLA Ops:
  0.6 1.7 %copy-start.2 = (bf16[40,4,4,8,192]{4,3,2,1,0:T(8,128)(2,1)S(1)}, bf16[40,4,4,8,192]{4,3,2,1,0:T(8,128)(2,1)}, u32[]{:S(2)}) copy-start(bf16[40,4,4,8,192]{4,3,2,1,0:T(8,128)(2,1)} %param.4) | copy-start | bytes 5898244
  3.7 1.3 %copy-start = (bf16[7680,128]{1,0:T(8,128)(2,1)}, bf16[7680,128]{1,0:T(8,128)(2,1)S(1)}, u32[]{:S(2)}) copy-start(bf16[7680,128]{1,0:T(8,128)(2,1)S(1)} %pack.1) | copy-start | bytes 5898244
  5.0 7.5 %copy-start.6 = (s32[640]{0:T(1024)S(1)}, s32[640]{0:T(1024)}, u32[]{:S(2)}) copy-start(s32[640]{0:T(1024)} %param.5) | copy-start | bytes 7684
  5.0 7.7 %copy-start.1 = (f32[4,8,12,640]{3,1,2,0:T(8,128)S(1)}, f32[4,8,12,640]{3,1,2,0:T(8,128)}, u32[]{:S(2)}) copy-start(f32[4,8,12,640]{3,1,2,0:T(8,128)} %param.6) | copy-start | bytes 2949124
  5.0 46.4 %copy-start.5 = (f32[8,640]{1,0:T(8,128)S(1)}, f32[8,640]{1,0:T(8,128)}, u32[]{:S(2)}) copy-start(f32[8,640]{1,0:T(8,128)} %weight_ref.1) | copy-start | bytes 61444
  5.0 46.4 %all-to-all-start = ((bf16[16,480,128]{2,1,0:T(8,128)(2,1)}), bf16[16,480,128]{2,1,0:T(8,128)(2,1)S(1)}, u32[]{:S(2)}, u32[]{:S(2)}) async-start(bf16[16,480,128]{2,1,0:T(8,128)(2,1)} %bitcast.4), calls=%async_computation | async-start | bytes 3932160 | tf_op jit(solution)/shard_map/all_to_all | solution.py:280
  13.1 0.9 copy-start.3
  51.3 1.1 %copy-start.4 = (bf16[640,640]{1,0:T(8,128)(2,1)S(1)}, bf16[640,640]{1,0:T(8,128)(2,1)}, u32[]{:S(2)}) copy-start(bf16[640,640]{1,0:T(8,128)(2,1)} %copy-done.3) | copy-start | bytes 2457604

commit v2 on v1

--- a/solution.py
+++ b/solution.py
@@ -17,46 +17,20 @@
     return [(a, b) for a in range(kept) for b in range(a, kept)]
 
 
-def pack_kernel(rows, t_ref, out_ref, wide):
-    lons = t_ref.shape[2]
-    eye = (
-        lax.broadcasted_iota(jnp.int32, (lons, lons), 0)
-        == lax.broadcasted_iota(jnp.int32, (lons, lons), 1)
-    ).astype(F32).astype(BF16)
-    for r in range(rows):
-        turned = lax.dot_general(
-            eye, t_ref[r], (((1,), (1,)), ((), ())), preferred_element_type=F32
-        )
-        wide[pl.ds(r, lons, stride=rows), :] = turned
-    out_ref[...] = wide[...].astype(BF16)
-
-
 def row_sum(cells):
     total = jnp.sum(jnp.sum(cells, axis=0), axis=0, keepdims=True)
     return sum(total[:, at : at + 128] for at in range(0, total.shape[1], 128))
 
 
-def prep_kernel(lat_ref, basis_ref, perm_ref, gram_ref):
-    lats = perm_ref.shape[0]
-    kept = basis_ref.shape[0]
-    perm_ref[...] = (
-        (lat_ref[...] == lax.broadcasted_iota(jnp.int32, (lats, lats), 1))
-        .astype(F32)
-        .astype(BF16)
-    )
-    gram_ref[...] = jnp.zeros_like(gram_ref)
-    for at, (a, b) in enumerate(pairs(kept)):
-        gram_ref[kept + 1 + at : kept + 2 + at, :] = row_sum(basis_ref[a] * basis_ref[b])
-
-
 def main_kernel(
-    count, rows, cells, recv_ref, perm_ref, basis_ref, weight_ref, gram_ref,
+    count, rows, cells, fused, source_ref, lat_ref, basis_hbm, weight_ref,
     out_ref, coef_ref,
-    wide, coefs, state, halo, edge, gathered,
-    halo_send, halo_recv, sum_send, sum_recv,
+    wide, coefs, state, halo, edge, gathered, perm, basis_ref,
+    halo_send, halo_recv, sum_send, sum_recv, load_sem, *more,
 ):
     kept, tile, levels, lats = basis_ref.shape
     steps = coefs.shape[0]
+    quads = tile // 4
     me = lax.axis_index("lon")
     west = lax.rem(me + count - 1, count)
     east = lax.rem(me + 1, count)
@@ -69,7 +43,12 @@
             device_id_type=pl.DeviceIdType.MESH,
         )
 
-    wide[...] = recv_ref[...].astype(F32)
+    load_last = pltpu.make_async_copy(
+        basis_hbm.at[kept - 1], basis_ref.at[kept - 1], load_sem.at[0]
+    )
+    load_rest = pltpu.make_async_copy(
+        basis_hbm.at[0 : kept - 1], basis_ref.at[0 : kept - 1], load_sem.at[1]
+    )
     level = lax.broadcasted_iota(jnp.int32, (levels, lats), 0)
     lat = lax.broadcasted_iota(jnp.int32, (levels, lats), 1)
     up = (level < levels - 1).astype(F32)
@@ -77,23 +56,24 @@
     not_north = (lat < lats - 1).astype(F32)
     not_south = (lat > 0).astype(F32)
 
-    def fields(i, _):
-        block = wide[:, pl.ds(pl.multiple_of(i * rows, 8), rows), :]
-        block = block.reshape(lats, block.shape[2]).astype(BF16)
-        raw = lax.dot_general(
-            block, perm_ref[...], (((0,), (0,)), ((), ())), preferred_element_type=F32
-        ).reshape(steps, 4, levels, lats)
-        u = 0.1 * jnp.tanh(raw[:, 0])
-        v = 0.1 * jnp.tanh(raw[:, 1])
-        k = 0.095 + 0.055 * jnp.tanh(0.5 * raw[:, 2])
-        m = 0.06 + 0.04 * jnp.tanh(0.5 * raw[:, 3])
-        coefs[:, 0, i] = 1.0 - 4.0 * k - 2.0 * m
-        coefs[:, 1, i] = k - u
-        coefs[:, 2, i] = k + u
-        coefs[:, 3, i] = (k - v) * not_north
-        coefs[:, 4, i] = (k + v) * not_south
-        coefs[:, 5, i] = m
-        return 0
+    def fields(s):
+        for quad in range(quads):
+            at = (s * quads + quad) * rows
+            block = wide[:, at : at + rows, :].reshape(lats, 128).astype(BF16)
+            raw = lax.dot_general(
+                block, perm[...], (((0,), (0,)), ((), ())), preferred_element_type=F32
+            ).reshape(4, 4, levels, lats)
+            u = 0.1 * jnp.tanh(raw[:, 0])
+            v = 0.1 * jnp.tanh(raw[:, 1])
+            k = 0.095 + 0.055 * jnp.tanh(0.5 * raw[:, 2])
+            m = 0.06 + 0.04 * jnp.tanh(0.5 * raw[:, 3])
+            cols = slice(4 * quad, 4 * quad + 4)
+            coefs[s, 0, cols] = 1.0 - 4.0 * k - 2.0 * m
+            coefs[s, 1, cols] = k - u
+            coefs[s, 2, cols] = k + u
+            coefs[s, 3, cols] = (k - v) * not_north
+            coefs[s, 4, cols] = (k + v) * not_south
+            coefs[s, 5, cols] = m
 
     def copies(slot):
         return [
@@ -149,17 +129,127 @@
             + roll(up * d, 1, 1)
         )
 
-    half = tile // 2
-    lax.fori_loop(0, half, fields, 0)
-    pl.semaphore_wait(barrier, count - 1)
-    state[0] = basis_ref[kept - 1]
-    send(0, state[0, 0], state[0, tile - 1])
-    lax.fori_loop(half, tile, fields, 0)
+    def prepare():
+        perm[...] = jnp.transpose(
+            (lax.broadcasted_iota(jnp.int32, (lats, lats), 0) == lat_ref[...]).astype(F32)
+        ).astype(BF16)
+        gathered[me] = jnp.zeros((16, 128), F32)
+        for at, (a, b) in enumerate(pairs(kept)):
+            gathered[me, kept + 1 + at : kept + 2 + at, :] = row_sum(basis_ref[a] * basis_ref[b])
+
+    def start_state():
+        load_last.wait()
+        state[0] = basis_ref[kept - 1]
+        send(0, state[0, 0], state[0, tile - 1])
+
+    if fused:
+        raw_ref, turned, outbox, inbox, raw_sem, box_send, box_recv = more
+        lanes, lons = raw_ref.shape[2], raw_ref.shape[3]
+        per_step = quads * rows
+        bounds = [-(-s * per_step // 16) * 16 for s in range(steps + 1)]
+        loads = [
+            pltpu.make_async_copy(
+                source_ref.at[:, s * lanes : (s + 1) * lanes], raw_ref.at[s], raw_sem.at[s]
+            )
+            for s in range(steps)
+        ]
+        loads[0].start()
+        load_last.start()
+        for load in loads[1:]:
+            load.start()
+        load_rest.start()
+        row = lax.broadcasted_iota(jnp.int32, (4 * lanes, lons), 0)
+        lon = lax.broadcasted_iota(jnp.int32, (4 * lanes, lons), 1)
+        quarter = lon & 3
+        keep = sum(
+            ((row >= lanes * q) & (row < lanes * (q + 1)) & (quarter == q)).astype(F32)
+            for q in range(4)
+        ).astype(BF16)
+        row = lax.broadcasted_iota(jnp.int32, (lons // 4, lons), 0)
+        lon = lax.broadcasted_iota(jnp.int32, (lons // 4, lons), 1)
+        pick = ((lon >= 4 * row) & (lon < 4 * row + 4)).astype(F32).astype(BF16)
+
+        def turn(s, lo, hi):
+            for r in range(lo, hi):
+                a = raw_ref[s, r]
+                a = jnp.concatenate([a, a, a, a], axis=0) * keep
+                turned[pl.ds(s * count * per_step + r, lons // 4, stride=rows), :] = (
+                    lax.dot_general(
+                        pick, a, (((1,), (1,)), ((), ())), preferred_element_type=F32
+                    )
+                )
+
+        def step_rows(s, lo, hi):
+            whole = turned[s * count * per_step : (s + 1) * count * per_step]
+            return whole.reshape(count, per_step, 128)[:, lo:hi]
+
+        def pack(p):
+            lo, hi = bounds[p], bounds[p + 1]
+            parts = [step_rows(p, lo - p * per_step, per_step)]
+            if hi > (p + 1) * per_step:
+                parts.append(step_rows(p + 1, 0, hi - (p + 1) * per_step))
+            outbox[:, lo:hi] = jnp.concatenate(parts, axis=1).astype(BF16)
+            inbox[me, lo:hi] = outbox[me, lo:hi]
+
+        def box(p, target, source, d):
+            lo, hi = bounds[p], bounds[p + 1]
+            return pltpu.make_async_remote_copy(
+                src_ref=outbox.at[target, lo:hi],
+                dst_ref=inbox.at[source, lo:hi],
+                send_sem=box_send.at[p, d],
+                recv_sem=box_recv.at[p, source],
+                device_id={"lon": target},
+                device_id_type=pl.DeviceIdType.MESH,
+            )
+
+        def post(p):
+            @pl.loop(1, count)
+            def _(d):
+                box(p, lax.rem(me + d, count), me, d).start()
+
+        def arrive(p):
+            @pl.loop(1, count)
+            def _(d):
+                source = lax.rem(me + d, count)
+                box(p, source, source, d).wait_recv()
+
+            lo, hi = bounds[p], bounds[p + 1]
+            wide[:, lo:hi] = inbox[:, lo:hi].astype(F32)
+
+        loads[0].wait()
+        turn(0, 0, rows)
+        loads[1].wait()
+        turn(1, 0, 8)
+        pack(0)
+        pl.semaphore_wait(barrier, count - 1)
+        start_state()
+        post(0)
+        turn(1, 8, rows)
+        pack(1)
+        post(1)
+        for s in range(2, steps):
+            loads[s].wait()
+            turn(s, 0, rows)
+        for s in range(2, steps):
+            pack(s)
+        load_rest.wait()
+        prepare()
+    else:
+        load_last.start()
+        load_rest.start()
+        wide[...] = source_ref[...].astype(F32)
+        pl.semaphore_wait(barrier, count - 1)
+        start_state()
+        load_rest.wait()
+        prepare()
 
     for t in range(2 * steps):
         now, new = t % 2, (t + 1) % 2
         if t < steps:
             s = t
+            if fused:
+                arrive(t)
+            fields(t)
             inside = forward(
                 s, 1, tile - 1, state[now, 1 : tile - 1],
                 state[now, 2:tile], state[now, 0 : tile - 2],
@@ -197,10 +287,11 @@
         state[new, 0:1] = first
         state[new, tile - 1 : tile] = last
         state[new, 1 : tile - 1] = inside
+        if fused and t + 2 < steps:
+            post(t + 2)
 
     w = state[0]
     own = [row_sum(basis_ref[k] * w) for k in range(kept)] + [row_sum(w * w)]
-    gathered[me] = gram_ref[...]
     for k in range(kept + 1):
         gathered[me, k : k + 1, :] = own[k]
 
@@ -237,10 +328,11 @@
         g = total[kept + 1 + at : kept + 2 + at]
         square = square + (1.0 if a == b else 2.0) * c[a] * c[b] * g
     beta = jnp.sqrt(square + 1e-06)
-    for k in range(kept):
-        coef_ref[k : k + 1, :] = jnp.broadcast_to(c[k], (1, 128))
-    coef_ref[kept : kept + 1, :] = jnp.broadcast_to(beta, (1, 128))
-    coef_ref[kept + 1 :, :] = jnp.zeros((8 - kept - 1, 128), F32)
+    lane = lax.broadcasted_iota(jnp.int32, (8, 128), 1)
+    coef_ref[...] = sum(
+        jnp.where(lane == k, jnp.broadcast_to(x, (8, 128)), 0.0)
+        for k, x in enumerate(c + [beta])
+    )
     scale = jnp.broadcast_to(1.0 / beta, (levels, lats))
     full = [jnp.broadcast_to(x, (levels, lats)) for x in c]
     for i in range(tile):
@@ -257,6 +349,13 @@
     def _(d):
         share(d).wait_send()
 
+    if fused:
+        for p in range(steps):
+
+            @pl.loop(1, count)
+            def _(d, p=p):
+                box(p, lax.rem(me + d, count), me, d).wait_send()
+
 
 def shards(trajectory, lat_order, basis, weight):
     rows, steps, states, levels, lons = trajectory.shape
@@ -265,67 +364,57 @@
     lanes = steps * states * levels
     cells = float(levels * lons * lats)
     flat = trajectory.reshape(rows, lanes, lons)
-    if rows % 8 == 0:
-        packed = pl.pallas_call(
-            functools.partial(pack_kernel, rows),
-            out_shape=jax.ShapeDtypeStruct((lons * rows, lanes), BF16),
-            in_specs=[VMEM],
-            out_specs=VMEM,
-            scratch_shapes=[pltpu.VMEM((lons * rows, lanes), F32)],
-            compiler_params=pltpu.CompilerParams(vmem_limit_bytes=24 * MIB),
-            name="pack",
-        )(flat)
+    quads = tile // 4
+    fused = rows % 8 == 0 and (steps * quads * rows) % 16 == 0 and steps % 2 == 0
+    slots = 2 * steps
+    more = []
+    if fused:
+        source, place, blocks, run = flat, pl.BlockSpec(memory_space=pl.ANY), count, rows
+        more = [
+            pltpu.VMEM((steps, rows, lanes // steps, lons), BF16),
+            pltpu.VMEM((lons * rows, lanes), F32),
+            pltpu.VMEM((count, tile * rows, lanes), BF16),
+            pltpu.VMEM((count, tile * rows, lanes), BF16),
+            pltpu.SemaphoreType.DMA((steps,)),
+            pltpu.SemaphoreType.DMA((steps, count)),
+            pltpu.SemaphoreType.DMA((steps, count)),
+        ]
     else:
-        packed = jnp.transpose(flat, (2, 0, 1))
-    received = lax.all_to_all(
-        packed.reshape(count, tile * rows, lanes), "lon", split_axis=0, concat_axis=0, tiled=True
-    )
-    if rows % 8:
-        received = jnp.transpose(received.reshape(count, tile, rows, lanes), (1, 0, 2, 3))
-        received = received.reshape(1, tile * lats, lanes)
-        rows = lats
-    turned = jnp.transpose(basis, (0, 2, 1, 3))
-    perm, gram = pl.pallas_call(
-        prep_kernel,
-        out_shape=(
-            jax.ShapeDtypeStruct((lats, lats), BF16),
-            jax.ShapeDtypeStruct((16, 128), F32),
-        ),
-        in_specs=[VMEM] * 2,
-        out_specs=(VMEM, VMEM),
-        cost_estimate=pl.CostEstimate(
-            flops=20_000_000, bytes_accessed=4_000_000, transcendentals=0
-        ),
-        compiler_params=pltpu.CompilerParams(vmem_limit_bytes=16 * MIB),
-        name="prepare",
-    )(lat_order[:, None], turned)
-    slots = 2 * steps
+        packed = jnp.transpose(flat, (2, 0, 1)).reshape(count, tile * rows, lanes)
+        got = lax.all_to_all(packed, "lon", split_axis=0, concat_axis=0, tiled=True)
+        got = got.reshape(count, quads, 4, rows, steps, lanes // steps)
+        got = jnp.transpose(got, (4, 1, 0, 3, 2, 5))
+        source, place, blocks, run = got.reshape(1, tile * lats, lanes), VMEM, 1, lats
     out, coef = pl.pallas_call(
-        functools.partial(main_kernel, count, rows, cells),
+        functools.partial(main_kernel, count, run, cells, fused),
         out_shape=(
             jax.ShapeDtypeStruct((tile, levels, lats), F32),
             jax.ShapeDtypeStruct((8, 128), F32),
         ),
-        in_specs=[VMEM] * 5,
+        in_specs=[place, VMEM, pl.BlockSpec(memory_space=pl.ANY), VMEM],
         out_specs=(VMEM, VMEM),
         scratch_shapes=[
-            pltpu.VMEM(received.shape, F32),
+            pltpu.VMEM((blocks, tile * run, lanes), F32),
             pltpu.VMEM((steps, 6, tile, levels, lats), F32),
             pltpu.VMEM((2, tile, levels, lats), F32),
             pltpu.VMEM((slots, 2, levels, lats), F32),
             pltpu.VMEM((slots, 2, levels, lats), F32),
             pltpu.VMEM((count, 16, 128), F32),
+            pltpu.VMEM((lats, lats), BF16),
+            pltpu.VMEM((kept, tile, levels, lats), F32),
             pltpu.SemaphoreType.DMA((slots, 2)),
             pltpu.SemaphoreType.DMA((slots, 2)),
             pltpu.SemaphoreType.DMA((count,)),
             pltpu.SemaphoreType.DMA((count,)),
-        ],
+            pltpu.SemaphoreType.DMA((2,)),
+        ]
+        + more,
         compiler_params=pltpu.CompilerParams(
-            collective_id=0, has_side_effects=True, vmem_limit_bytes=40 * MIB
+            collective_id=0, has_side_effects=True, vmem_limit_bytes=63 * MIB
         ),
         name="iterate",
-    )(received, perm, turned, weight, gram)
-    return jnp.transpose(out, (1, 0, 2)), coef[: kept + 1, 0]
+    )(source, lat_order[None], jnp.transpose(basis, (0, 2, 1, 3)), weight)
+    return jnp.transpose(out, (1, 0, 2)), coef[0, : kept + 1]
 
 
 def solution(mesh):

time: 98.4 us -> 79.7 us (0.81)
  waiting for transfers between devices: 37.3 us -> 0 us
  Pallas kernels: 46.1 us -> 74.7 us
  starting transfers between devices: 7.52 us -> 0 us
  local copies, waits for them, and re-layouts: 6.57 us -> 4.11 us
    all_to_all x1 -> x0, waiting for transfers between devices: 37.3 us -> none  [shards(): lax.all_to_all(packed.reshape(count, tile * rows, lanes), 'lon', split_ax...]
    pallas_call x3 -> x1, Pallas kernels: 46.1 us -> 74.7 us  [shards(): pl.pallas_call(functools.partial(main_kernel, count, run, cells, fused),...]
    all_to_all x1 -> x0, starting transfers between devices: 7.52 us -> none  [shards(): lax.all_to_all(packed.reshape(count, tile * rows, lanes), 'lon', split_ax...]
    unnamed x15 -> x1, local copies, waits for them, and re-layouts: 5.8 us -> 1.65 us
    squeeze x0 -> x1, local copies, waits for them, and re-layouts: none -> 1.19 us  [shards(): return (jnp.transpose(out, (1, 0, 2)), coef[0, :kept + 1])]
    broadcast_in_dim x1, local copies, waits for them, and re-layouts: 0.14 us -> 1.27 us  [shards(): lat_order[None]]
  transfers between devices with their start and end apart: 1 -> 0, of which waited for: 1 -> 0; matrix products, arithmetic and copies ran while one was open for 0% -> 0% of each run, Pallas kernels for 0% -> 0%
where the time goes in v2:
time: 79.7 us; the launch traced here: 79.4 us
  Pallas kernels  74.7 us (94%)
  local copies, waits for them, and re-layouts  4.11 us (5%)
    pallas_call x1, Pallas kernels, shards(): pl.pallas_call(functools.partial(main_kernel, count, run, cells, fused),...  74.7 us
    unnamed x1, local copies, waits for them, and re-layouts  1.65 us

profile of v2, /device:TPU:0, one launch (start us, length us, event | category | flops | bytes accessed | tf_op | source)
XLA Modules:
  0.0 79.4 jit_solution(18385891889068751072)
XLA Ops:
  0.6 1.3 %broadcast_in_dim.3.lat_ref = s32[1,640]{1,0:T(1,128)} reshape(s32[640]{0:T(1024)} %param.5) | data formatting | bytes 5120 | tf_op jit(solution)/shard_map/broadcast_in_dim | solution.py:416
  1.9 74.7 %iterate.1 = (f32[12,8,640]{2,1,0:T(8,128)}, f32[8,128]{1,0:T(8,128)}) custom-call(bf16[40,128,192]{2,1,0:T(8,128)(2,1)} %bitcast.5, s32[1,640]{1,0:T(1,128)} %broadcast_in_dim.3.lat_ref, f32[4,12,8,640]{3,2,1,0:T(8,128)} %bitcast.6, f32[8,640]{1,0:T(8,128)} %weight_ref.1), custom_call_target="tpu_custom_call" | custom-call | tf_op jit(solution)/shard_map/iterate/pallas_call | solution.py:388
  76.6 1.2 %slice_bitcast_fusion = f32[5]{0:T(128)} fusion(f32[8,128]{1,0:T(8,128)} %get-tuple-element.5), kind=kLoop, calls=%fused_computation | loop fusion | bytes 40 | tf_op jit(solution)/shard_map/squeeze | solution.py:417
  77.8 1.7 %copy.7 = f32[8,12,640]{2,0,1:T(8,128)} copy(f32[8,12,640]{2,0,1:T(8,128)} %bitcast.7) | data formatting | bytes 491520

commit v3 on v2

--- a/solution.py
+++ b/solution.py
@@ -131,7 +131,7 @@
 
     def prepare():
         perm[...] = jnp.transpose(
-            (lax.broadcasted_iota(jnp.int32, (lats, lats), 0) == lat_ref[...]).astype(F32)
+            (lax.broadcasted_iota(jnp.int32, (lats, lats), 0) == lat_ref[...].reshape(1, lats)).astype(F32)
         ).astype(BF16)
         gathered[me] = jnp.zeros((16, 128), F32)
         for at, (a, b) in enumerate(pairs(kept)):
@@ -243,52 +243,68 @@
         load_rest.wait()
         prepare()
 
-    for t in range(2 * steps):
+    flux_slot = lambda k: steps + 3 * k
+    part_slot = lambda k: steps + 3 * k + 1
+    coef_slot = lambda k: steps + 3 * k + 2
+
+    for t in range(steps):
         now, new = t % 2, (t + 1) % 2
-        if t < steps:
-            s = t
-            if fused:
-                arrive(t)
-            fields(t)
-            inside = forward(
-                s, 1, tile - 1, state[now, 1 : tile - 1],
-                state[now, 2:tile], state[now, 0 : tile - 2],
-            )
-            he, hw = receive(t)
-            first = forward(s, 0, 1, state[now, 0:1], state[now, 1:2], hw)
-            last = forward(
-                s, tile - 1, tile, state[now, tile - 1 : tile], he,
-                state[now, tile - 2 : tile - 1],
-            )
-            if t == steps - 1:
-                inside = weight_ref[...] * inside
-                first = weight_ref[...] * first
-                last = weight_ref[...] * last
+        if fused:
+            arrive(t)
+        fields(t)
+        inside = forward(
+            t, 1, tile - 1, state[now, 1 : tile - 1],
+            state[now, 2:tile], state[now, 0 : tile - 2],
+        )
+        he, hw = receive(t)
+        first = forward(t, 0, 1, state[now, 0:1], state[now, 1:2], hw)
+        last = forward(
+            t, tile - 1, tile, state[now, tile - 1 : tile], he,
+            state[now, tile - 2 : tile - 1],
+        )
+        if t == steps - 1:
+            inside = weight_ref[...] * inside
+            first = weight_ref[...] * first
+            last = weight_ref[...] * last
         else:
-            s = 2 * steps - 1 - t
-            inside = adjoint(
-                s, 1, tile - 1, state[now, 1 : tile - 1],
-                coefs[s, 2, 2:tile] * state[now, 2:tile],
-                coefs[s, 1, 0 : tile - 2] * state[now, 0 : tile - 2],
-            )
-            he, hw = receive(t)
-            first = adjoint(
-                s, 0, 1, state[now, 0:1], coefs[s, 2, 1:2] * state[now, 1:2], hw
-            )
-            last = adjoint(
-                s, tile - 1, tile, state[now, tile - 1 : tile], he,
-                coefs[s, 1, tile - 2 : tile - 1] * state[now, tile - 2 : tile - 1],
-            )
-        if t < steps - 1:
             send(t + 1, first[0], last[0])
-        elif t < 2 * steps - 1:
-            s = 2 * steps - 2 - t
-            send(t + 1, coefs[s, 2, 0] * first[0], coefs[s, 1, tile - 1] * last[0])
         state[new, 0:1] = first
         state[new, tile - 1 : tile] = last
         state[new, 1 : tile - 1] = inside
+        if t % 2 == 0:
+            send(coef_slot((steps - 2 - t) // 2), coefs[t, 2, 0], coefs[t, 1, tile - 1])
         if fused and t + 2 < steps:
             post(t + 2)
+
+    none = jnp.zeros((1, levels, lats), F32)
+    for k in range(steps // 2):
+        s = steps - 1 - 2 * k
+        to_west = coefs[s, 2, 0:1] * state[0, 0:1]
+        to_east = coefs[s, 1, tile - 1 : tile] * state[0, tile - 1 : tile]
+        first = adjoint(s, 0, 1, state[0, 0:1], coefs[s, 2, 1:2] * state[0, 1:2], none)
+        last = adjoint(
+            s, tile - 1, tile, state[0, tile - 1 : tile], none,
+            coefs[s, 1, tile - 2 : tile - 1] * state[0, tile - 2 : tile - 1],
+        )
+        send(flux_slot(k), to_west[0], to_east[0])
+        send(part_slot(k), first[0], last[0])
+        state[1, 1 : tile - 1] = adjoint(
+            s, 1, tile - 1, state[0, 1 : tile - 1],
+            coefs[s, 2, 2:tile] * state[0, 2:tile],
+            coefs[s, 1, 0 : tile - 2] * state[0, 0 : tile - 2],
+        )
+        ce, cw = receive(coef_slot(k))
+        he, hw = receive(flux_slot(k))
+        pe, pw = receive(part_slot(k))
+        state[1, 0:1] = first + hw
+        state[1, tile - 1 : tile] = last + he
+        he = ce * (pe + to_east)
+        hw = cw * (pw + to_west)
+        s = s - 1
+        y = state[1]
+        fe = jnp.concatenate([coefs[s, 2, 1:tile] * y[1:tile], he], axis=0)
+        fw = jnp.concatenate([hw, coefs[s, 1, 0 : tile - 1] * y[0 : tile - 1]], axis=0)
+        state[0] = adjoint(s, 0, tile, y, fe, fw)
 
     w = state[0]
     own = [row_sum(basis_ref[k] * w) for k in range(kept)] + [row_sum(w * w)]
@@ -341,7 +357,7 @@
             r = r - full[k] * basis_ref[k, i]
         out_ref[i] = r * scale
 
-    for t in range(2 * steps):
+    for t in range(steps + 3 * (steps // 2)):
         for copy in copies(t):
             copy.wait_send()
 
@@ -366,7 +382,7 @@
     flat = trajectory.reshape(rows, lanes, lons)
     quads = tile // 4
     fused = rows % 8 == 0 and (steps * quads * rows) % 16 == 0 and steps % 2 == 0
-    slots = 2 * steps
+    slots = steps + 3 * (steps // 2)
     more = []
     if fused:
         source, place, blocks, run = flat, pl.BlockSpec(memory_space=pl.ANY), count, rows
@@ -413,7 +429,7 @@
             collective_id=0, has_side_effects=True, vmem_limit_bytes=63 * MIB
         ),
         name="iterate",
-    )(source, lat_order[None], jnp.transpose(basis, (0, 2, 1, 3)), weight)
+    )(source, lat_order, jnp.transpose(basis, (0, 2, 1, 3)), weight)
     return jnp.transpose(out, (1, 0, 2)), coef[0, : kept + 1]
 
 

time: 79.7 us -> 72.2 us (0.906)
  Pallas kernels: 74.7 us -> 68.5 us
  local copies, waits for them, and re-layouts: 4.11 us -> 2.84 us
    pallas_call x1, Pallas kernels: 74.7 us -> 68.5 us  [shards(): pl.pallas_call(functools.partial(main_kernel, count, run, cells, fused),...]
    broadcast_in_dim x1 -> x0, local copies, waits for them, and re-layouts: 1.27 us -> none  [shards(): lat_order[None]]
where the time goes in v3:
time: 72.2 us; the launch traced here: 72 us
  Pallas kernels  68.5 us (95%)
  local copies, waits for them, and re-layouts  2.84 us (4%)
    pallas_call x1, Pallas kernels, shards(): pl.pallas_call(functools.partial(main_kernel, count, run, cells, fused),...  68.5 us
    unnamed x1, local copies, waits for them, and re-layouts  1.65 us

profile of v3, /device:TPU:0, one launch (start us, length us, event | category | flops | bytes accessed | tf_op | source)
XLA Modules:
  0.0 72.0 jit_solution(606157922009199382)
XLA Ops:
  0.6 68.5 %iterate.1 = (f32[12,8,640]{2,1,0:T(8,128)}, f32[8,128]{1,0:T(8,128)}) custom-call(bf16[40,128,192]{2,1,0:T(8,128)(2,1)} %bitcast.5, s32[640]{0:T(1024)} %lat_ref.1, f32[4,12,8,640]{3,2,1,0:T(8,128)} %bitcast.6, f32[8,640]{1,0:T(8,128)} %weight_ref.1), custom_call_target="tpu_custom_call" | custom-call | tf_op jit(solution)/shard_map/iterate/pallas_call | solution.py:404
  69.2 1.2 %slice_bitcast_fusion = f32[5]{0:T(128)} fusion(f32[8,128]{1,0:T(8,128)} %get-tuple-element.5), kind=kLoop, calls=%fused_computation | loop fusion | bytes 40 | tf_op jit(solution)/shard_map/squeeze | solution.py:433
  70.4 1.7 %copy.7 = f32[8,12,640]{2,0,1:T(8,128)} copy(f32[8,12,640]{2,0,1:T(8,128)} %bitcast.7) | data formatting | bytes 491520

commit v4 on v3

--- a/solution.py
+++ b/solution.py
@@ -205,7 +205,8 @@
         def post(p):
             @pl.loop(1, count)
             def _(d):
-                box(p, lax.rem(me + d, count), me, d).start()
+                at = lax.rem(d + count // 2 - 2, count - 1) + 1
+                box(p, lax.rem(me + at, count), me, at).start()
 
         def arrive(p):
             @pl.loop(1, count)

time: 72.2 us -> 71.3 us (0.988)
  Pallas kernels: 68.5 us -> 67.6 us
    pallas_call x1, Pallas kernels: 68.5 us -> 67.6 us  [shards(): pl.pallas_call(functools.partial(main_kernel, count, run, cells, fused),...]
where the time goes in v4:
time: 71.3 us; the launch traced here: 71.1 us
  Pallas kernels  67.6 us (95%)
  local copies, waits for them, and re-layouts  2.84 us (4%)
    pallas_call x1, Pallas kernels, shards(): pl.pallas_call(functools.partial(main_kernel, count, run, cells, fused),...  67.6 us
    unnamed x1, local copies, waits for them, and re-layouts  1.65 us

profile of v4, /device:TPU:0, one launch (start us, length us, event | category | flops | bytes accessed | tf_op | source)
XLA Modules:
  0.0 71.1 jit_solution(7115177737400571776)
XLA Ops:
  0.6 67.6 %iterate.1 = (f32[12,8,640]{2,1,0:T(8,128)}, f32[8,128]{1,0:T(8,128)}) custom-call(bf16[40,128,192]{2,1,0:T(8,128)(2,1)} %bitcast.5, s32[640]{0:T(1024)} %lat_ref.1, f32[4,12,8,640]{3,2,1,0:T(8,128)} %bitcast.6, f32[8,640]{1,0:T(8,128)} %weight_ref.1), custom_call_target="tpu_custom_call" | custom-call | tf_op jit(solution)/shard_map/iterate/pallas_call | solution.py:405
  68.2 1.2 %slice_bitcast_fusion = f32[5]{0:T(128)} fusion(f32[8,128]{1,0:T(8,128)} %get-tuple-element.5), kind=kLoop, calls=%fused_computation | loop fusion | bytes 40 | tf_op jit(solution)/shard_map/squeeze | solution.py:434
  69.4 1.7 %copy.7 = f32[8,12,640]{2,0,1:T(8,128)} copy(f32[8,12,640]{2,0,1:T(8,128)} %bitcast.7) | data formatting | bytes 491520
